TPU v7x, 32 devices: a whole 2x2x4 slice. The times are simulated.
32 devices in a mesh: vid: 4 (over z), ty: 2 (over y), tx: 4 (over x, core).
Axes of the slice: x: 2, y: 2, z: 4, core: 2. Of those that a mesh axis runs over, the one named last changes fastest.
Arguments:
- latent_shards: bfloat16 [4, 99328], P('vid', ('ty', 'tx')), may hold values from -6 to 6
- shard_starts: int32 [4, 9], P('vid'), may hold values from 0 to 4096, as said below
- frame_dims: int32 [4, 2], P('vid'), may hold values from 16 to 128, as said below
- latent_cache: bfloat16 [4, 2, 32, 2048], P('vid', None, 'ty', 'tx'), may hold values from -6 to 6
- feature_cache: bfloat16 [4, 2, 32, 49152], P('vid', None, 'ty', 'tx'), may hold values from -5 to 5
- in_weight: bfloat16 [432, 384], replicated, may hold values from -0.3125 to 0.3125
- in_bias: float32 [384], replicated, may hold values from -3 to 3
- norm_gain: float32 [384], replicated, may hold values from 0.1 to 1.9
- res_weight: bfloat16 [10368, 384], replicated, may hold values from -0.0625 to 0.0625
- res_bias: float32 [384], replicated, may hold values from -3 to 3
- up_weight: bfloat16 [3456, 192], replicated, may hold values from -0.109375 to 0.109375
- up_bias: float32 [192], replicated, may hold values from -3 to 3
Outputs:
- decoded: bfloat16 [4, 64, 49152], P('vid', 'ty', 'tx')
Inputs may be any that keep to these rules, and one draw needn't show every extreme that they name: `frame_dims`: row i gives video i's height, from 16 to 32, and width, from 64 to 128; one video fills the whole canvas and another is exactly 16 by 64. `shard_starts`: row i starts at 0, never falls, ends at video i's height times width, and every shard's token count fits its 776 slots; tokens lie in row-major order of the frame.
All inputs are finite; a program needn't handle non-finite values.
Results may differ from a plain program's by a relative error of at most 0.0095.
Values may be sent and summed in bfloat16 or wider, within the bound.
A program may use at most 64 MiB of HBM per device.

v0:
```python
import jax
import jax.numpy as jnp
from jax import lax
from jax.sharding import PartitionSpec as P

EPS = 1e-06


def padded_2(value, sides, width):
    for axis, dim in sides:
        size, length = (lax.axis_size(axis), value.shape[dim])
        up = [(i, (i + 1) % size) for i in range(size - 1)]
        down = [(j, i) for i, j in up]
        last = lax.slice_in_dim(value, length - width, length, axis=dim)
        leading = lax.slice_in_dim(value, 0, width, axis=dim)
        before = lax.ppermute(last, axis, up)
        after = lax.ppermute(leading, axis, down)
        value = jnp.concatenate([before, value, after], axis=dim)
    return value


def tap_sum(padded, weight, row_count, col_count):
    channels = padded.shape[-1]
    summed = jnp.zeros((row_count * col_count, weight.shape[1]), jnp.float32)
    for frame_at in range(padded.shape[0]):
        for row_at in range(3):
            for col_at in range(3):
                tap_index = (frame_at * 3 + row_at) * 3 + col_at
                window = padded[
                    frame_at, row_at : row_at + row_count, col_at : col_at + col_count
                ].reshape(row_count * col_count, channels)
                summed = summed + jnp.dot(
                    window,
                    weight[tap_index * channels : (tap_index + 1) * channels],
                    preferred_element_type=jnp.float32,
                )
    return summed


def unfold_taps(padded, row_count, col_count):
    pieces = []
    for frame_at in range(padded.shape[0]):
        for row_at in range(3):
            for col_at in range(3):
                pieces.append(
                    padded[frame_at, row_at : row_at + row_count, col_at : col_at + col_count]
                )
    joined = jnp.concatenate(pieces, axis=-1)
    return joined.reshape(row_count * col_count, joined.shape[-1])


def token_routes(first, count, breadth, slot_cap, tile_rows, tile_cols, across, shard_count):
    offset = jnp.arange(slot_cap, dtype=jnp.int32)
    position = first[..., None] + offset
    live = offset < count[..., None]
    glob_row = position // breadth
    glob_col = position % breadth
    owner = jnp.where(live, glob_row // tile_rows * across + glob_col // tile_cols, shard_count)
    place = glob_row % tile_rows * tile_cols + glob_col % tile_cols
    return (owner, place)


def per_device(
    latent_shards,
    shard_starts,
    frame_dims,
    latent_cache,
    feature_cache,
    in_weight,
    in_bias,
    norm_gain,
    res_weight,
    res_bias,
    up_weight,
    up_bias,
):
    channels = in_bias.shape[0]
    latent_width = in_weight.shape[0] // 27
    out_width = up_bias.shape[0]
    tile_rows = feature_cache.shape[2]
    tile_cols = feature_cache.shape[3] // channels
    tile_cells = tile_rows * tile_cols
    across = lax.axis_size("tx")
    down_count = lax.axis_size("ty")
    shard_count = down_count * across
    row_index = lax.axis_index("ty")
    col_index = lax.axis_index("tx")
    myself = row_index * across + col_index
    height = frame_dims[0, 0]
    breadth = frame_dims[0, 1]
    starts = shard_starts[0]
    slot_cap = latent_shards.shape[1] // latent_width
    everything = lax.all_gather(latent_shards, ("ty", "tx"), axis=1, tiled=True).reshape(
        shard_count * slot_cap, latent_width
    )
    owner, place = token_routes(
        starts[:-1],
        starts[1:] - starts[:-1],
        breadth,
        slot_cap,
        tile_rows,
        tile_cols,
        across,
        shard_count,
    )
    target = jnp.where(owner == myself, place, tile_cells).reshape(-1)
    current = (
        jnp.zeros((tile_cells, latent_width), jnp.bfloat16).at[target].set(everything, mode="drop")
    )
    ycoord = row_index * tile_rows + jnp.arange(tile_rows, dtype=jnp.int32)
    xcoord = col_index * tile_cols + jnp.arange(tile_cols, dtype=jnp.int32)
    keep = ((ycoord[:, None] < height) & (xcoord[None, :] < breadth)).astype(jnp.float32)
    keep_low = keep.astype(jnp.bfloat16)[None, :, :, None]
    keep_flat = keep.reshape(-1, 1)
    lat_stack = (
        jnp.concatenate(
            [
                latent_cache[0].reshape(2, tile_rows, tile_cols, latent_width),
                current.reshape(1, tile_rows, tile_cols, latent_width),
            ],
            0,
        )
        * keep_low
    )
    lat_padded = padded_2(lat_stack, (("ty", 1), ("tx", 2)), 1)
    unfolded = unfold_taps(lat_padded, tile_rows, tile_cols)
    first_out = (jnp.dot(unfolded, in_weight, preferred_element_type=jnp.float32) + in_bias).astype(
        jnp.bfloat16
    )
    values = first_out.astype(jnp.float32)
    power = jnp.mean(values * values, axis=1, keepdims=True)
    normed = values * lax.rsqrt(power + EPS) * norm_gain
    hidden = (jax.nn.silu(normed) * keep_flat).astype(jnp.bfloat16)
    feat_stack = jnp.concatenate(
        [
            feature_cache[0].reshape(2, tile_rows, tile_cols, channels) * keep_low,
            hidden.reshape(1, tile_rows, tile_cols, channels),
        ],
        0,
    )
    feat_padded = padded_2(feat_stack, (("ty", 1), ("tx", 2)), 1)
    branch = tap_sum(feat_padded, res_weight, tile_rows, tile_cols)
    mixed = (
        ((values + branch + res_bias) * keep_flat)
        .astype(jnp.bfloat16)
        .reshape(tile_rows, tile_cols, channels)
    )
    low_padded = padded_2(mixed, (("ty", 0), ("tx", 1)), 1)
    grown_padded = jnp.repeat(jnp.repeat(low_padded, 2, axis=0), 2, axis=1)[1:-1, 1:-1]
    result = tap_sum(grown_padded[None], up_weight, 2 * tile_rows, 2 * tile_cols) + up_bias
    keep_high = jnp.repeat(jnp.repeat(keep, 2, axis=0), 2, axis=1).reshape(-1, 1)
    return (
        (result * keep_high)
        .astype(jnp.bfloat16)
        .reshape(1, 2 * tile_rows, 2 * tile_cols * out_width)
    )


def solution(mesh):
    return jax.shard_map(
        per_device,
        mesh=mesh,
        in_specs=(
            P("vid", ("ty", "tx")),
            P("vid", None),
            P("vid", None),
            P("vid", None, "ty", "tx"),
            P("vid", None, "ty", "tx"),
            P(),
            P(),
            P(),
            P(),
            P(),
            P(),
            P(),
        ),
        out_specs=P("vid", "ty", "tx"),
        check_vma=False,
    )
```

profile of v0, /device:TPU:1, one launch (start us, length us, event | category | flops | bytes accessed | tf_op | source)
XLA Modules:
  0.0 160.1 jit_solution(8422800603614920463)
XLA Ops:
  7.5 11.2 %all_gather.3 = bf16[1,99328]{1,0:T(2,128)(2,1)S(1)} all-gather(bf16[1,12416]{1,0:T(2,128)(2,1)} %param.12), channel_id=1, replica_groups=mesh['vid'=4,'ty'=2,'tx'=4] {'ty','tx'}, dimensions={1}, use_global_device_ids=true | all-gather | bytes 223488 | tf_op jit(solution)/shard_map/all_gather | solution.py:93
  23.1 24.5 %scatter_custom_fusion = bf16[512,16]{1,0:T(8,128)(2,1)S(1)} fusion(s32[6208]{0:T(1024)S(1)} %fusion.97, bf16[6208,16]{1,0:T(8,128)(2,1)S(1)} %reshape.439, bf16[]{:T(256)} %constant.70.clone.1), kind=kCustom, calls=%fused_computation.159 | custom fusion | bytes 16386 | tf_op jit(solution)/shard_map/scatter | solution.py:108
  47.8 2.9 %collective-permute-start = (bf16[3,1,32,16]{3,2,1,0:T(8,128)(2,1)S(1)}, bf16[3,1,32,16]{3,2,1,0:T(8,128)(2,1)S(1)}, u32[]{:S(2)}, u32[]{:S(2)}) collective-permute-start(bf16[3,1,32,16]{3,2,1,0:T(8,128)(2,1)S(1)} %get-tuple-element.84), channel_id=1, source_target_pairs={{0,4},{1,5},{2,6},{3,7},{8,12},{9,13},{10,14},{11,15},{16,20},{17,... | collective-permute-start | bytes 9224 | tf_op jit(solution)/shard_map/ppermute | solution.py:16
  52.3 1.4 fusion.72
  53.7 1.5 collective-permute-done.1
  56.2 3.5 %collective-permute-start.3 = (bf16[3,18,1,16]{3,2,1,0:T(2,128)(2,1)}, bf16[3,18,1,16]{3,2,1,0:T(2,128)(2,1)}, u32[]{:S(2)}, u32[]{:S(2)}) collective-permute-start(bf16[3,18,1,16]{3,2,1,0:T(2,128)(2,1)} %get-tuple-element.68), channel_id=1, source_target_pairs={{1,0},{2,1},{3,2},{5,4},{6,5},{7,6},{9,8},{10,9},{11,10},{13,12},{... | collective-permute-start | bytes 5192 | tf_op jit(solution)/shard_map/ppermute | solution.py:17
  59.7 2.5 %collective-permute-start.2 = (bf16[3,18,1,16]{3,2,1,0:T(2,128)(2,1)}, bf16[3,18,1,16]{3,2,1,0:T(2,128)(2,1)}, u32[]{:S(2)}, u32[]{:S(2)}) collective-permute-start(bf16[3,18,1,16]{3,2,1,0:T(2,128)(2,1)} %get-tuple-element.69), channel_id=1, source_target_pairs={{0,1},{1,2},{2,3},{4,5},{5,6},{6,7},{8,9},{9,10},{10,11},{12,13},{... | collective-permute-start | bytes 5192 | tf_op jit(solution)/shard_map/ppermute | solution.py:16
  63.0 1.6 copy.41
  88.7 1.7 %multiply_reduce_fusion = (f32[512]{0:T(512)S(1)}, f32[512,384]{1,0:T(8,128)S(1)}) fusion(f32[384]{0:T(512)S(1)} %copy-done.16, bf16[512,432]{0,1:T(8,128)(2,1)} %constant_dynamic-update-slice_fusion, bf16[432,384]{1,0:T(8,128)(2,1)S(1)} %copy-done), kind=kOutput, calls=%fused_computation.50 | convolution fusion | flops 170851840 | bytes 1564160 | tf_op jit(solution)/shard_map/dot_general | solution.py:127
  90.8 2.3 %collective-permute-start.4 = (bf16[3,1,32,384]{3,2,1,0:T(8,128)(2,1)S(1)}, bf16[3,1,32,384]{3,2,1,0:T(8,128)(2,1)S(1)}, u32[]{:S(2)}, u32[]{:S(2)}) collective-permute-start(bf16[3,1,32,384]{3,2,1,0:T(8,128)(2,1)S(1)} %get-tuple-element.45), channel_id=1, source_target_pairs={{0,4},{1,5},{2,6},{3,7},{8,12},{9,13},{10,14},{11,15},{16,20},{17,... | collective-permute-start | bytes 221192 | tf_op jit(solution)/shard_map/ppermute | solution.py:16
  95.7 2.9 %collective-permute-done.5 = bf16[3,1,32,384]{3,2,1,0:T(8,128)(2,1)S(1)} collective-permute-done((bf16[3,1,32,384]{3,2,1,0:T(8,128)(2,1)S(1)}, bf16[3,1,32,384]{3,2,1,0:T(8,128)(2,1)S(1)}, u32[]{:S(2)}, u32[]{:S(2)}) %collective-permute-start.5) | collective-permute-done | bytes 73760 | tf_op jit(solution)/shard_map/ppermute | solution.py:17
  100.5 3.3 %collective-permute-start.6 = (bf16[3,18,1,384]{3,2,1,0:T(2,128)(2,1)S(1)}, bf16[3,18,1,384]{3,2,1,0:T(2,128)(2,1)S(1)}, u32[]{:S(2)}, u32[]{:S(2)}) collective-permute-start(bf16[3,18,1,384]{3,2,1,0:T(2,128)(2,1)S(1)} %get-tuple-element.34), channel_id=1, source_target_pairs={{0,1},{1,2},{2,3},{4,5},{5,6},{6,7},{8,9},{9,10},{10,11},{12,13},{... | collective-permute-start | bytes 124424 | tf_op jit(solution)/shard_map/ppermute | solution.py:16
  103.8 2.1 %collective-permute-start.7 = (bf16[3,18,1,384]{3,2,1,0:T(2,128)(2,1)S(1)}, bf16[3,18,1,384]{3,2,1,0:T(2,128)(2,1)S(1)}, u32[]{:S(2)}, u32[]{:S(2)}) collective-permute-start(bf16[3,18,1,384]{3,2,1,0:T(2,128)(2,1)S(1)} %get-tuple-element.35), channel_id=1, source_target_pairs={{1,0},{2,1},{3,2},{5,4},{6,5},{7,6},{9,8},{10,9},{11,10},{13,12},{... | collective-permute-start | bytes 124424 | tf_op jit(solution)/shard_map/ppermute | solution.py:17
  110.3 1.9 %maximum_maximum_fusion = (bf16[3,18,33,384]{3,2,1,0:T(8,128)(2,1)S(1)}, bf16[3,18,33,384]{3,2,1,0:T(8,128)(2,1)S(1)}) fusion(bf16[3,1,32,384]{3,2,1,0:T(8,128)(2,1)S(1)} %collective-permute-done.5, bf16[1,16,32,384]{3,2,1,0:T(8,128)(2,1)S(1)} %bitcast.185, bf16[2,16,32,384]{3,2,1,0:T(8,128)(2,1)S(1)} %bitcast_multiply_fusion, ...), kind=kLoop, calls=%fused_computation.13 | loop fusion | flops 13685760 | bytes 4147200 | tf_op jit(solution)/shard_map/concatenate | solution.py:18
  112.2 2.0 %fusion.101 = (bf16[1,16,32,384]{3,2,1,0:T(8,128)(2,1)}, bf16[1,16,32,384]{3,2,1,0:T(8,128)(2,1)}, bf16[1,16,32,384]{3,2,1,0:T(8,128)(2,1)S(1)}, bf16[1,16,32,38...) fusion(bf16[3,18,33,384]{3,2,1,0:T(8,128)(2,1)S(1)} %get-tuple-, ...), kind=kLoop, calls=%fused_computation.218 | loop fusion | bytes 14155776 | tf_op jit(solution)/shard_map/slice | solution.py:29
  123.3 1.4 collective-permute-start.8
  126.1 3.3 %collective-permute-done.9 = bf16[1,32,384]{2,1,0:T(8,128)(2,1)S(1)} collective-permute-done((bf16[1,32,384]{2,1,0:T(8,128)(2,1)S(1)}, bf16[1,32,384]{2,1,0:T(8,128)(2,1)S(1)}, u32[]{:S(2)}, u32[]{:S(2)}) %collective-permute-start.9) | collective-permute-done | bytes 24608 | tf_op jit(solution)/shard_map/ppermute | solution.py:17
  129.4 5.1 %collective-permute-start.10 = (bf16[18,1,384]{2,1,0:T(2,128)(2,1)S(1)}, bf16[18,1,384]{2,1,0:T(2,128)(2,1)S(1)}, u32[]{:S(2)}, u32[]{:S(2)}) collective-permute-start(bf16[18,1,384]{2,1,0:T(2,128)(2,1)S(1)} %get-tuple-element.48), channel_id=1, source_target_pairs={{0,1},{1,2},{2,3},{4,5},{5,6},{6,7},{8,9},{9,10},{10,11},{12,13},{... | collective-permute-start | bytes 41480 | tf_op jit(solution)/shard_map/ppermute | solution.py:16
  134.5 2.2 %collective-permute-start.11 = (bf16[18,1,384]{2,1,0:T(2,128)(2,1)S(1)}, bf16[18,1,384]{2,1,0:T(2,128)(2,1)S(1)}, u32[]{:S(2)}, u32[]{:S(2)}) collective-permute-start(bf16[18,1,384]{2,1,0:T(2,128)(2,1)S(1)} %get-tuple-element.49), channel_id=1, source_target_pairs={{1,0},{2,1},{3,2},{5,4},{6,5},{7,6},{9,8},{10,9},{11,10},{13,12},{... | collective-permute-start | bytes 41480 | tf_op jit(solution)/shard_map/ppermute | solution.py:17
  137.2 2.5 %collective-permute-done.11 = bf16[18,1,384]{2,1,0:T(2,128)(2,1)S(1)} collective-permute-done((bf16[18,1,384]{2,1,0:T(2,128)(2,1)S(1)}, bf16[18,1,384]{2,1,0:T(2,128)(2,1)S(1)}, u32[]{:S(2)}, u32[]{:S(2)}) %collective-permute-start.11) | collective-permute-done | bytes 13856 | tf_op jit(solution)/shard_map/ppermute | solution.py:17
  140.0 2.2 %broadcast_in_dim.42 = bf16[36,34,2,384]{3,2,1,0:T(2,128)(2,1)} broadcast(bf16[36,34,384]{2,1,0:T(8,128)(2,1)S(1)} %bitcast.197), dimensions={0,1,3} | broadcast | bytes 2820096 | tf_op jit(solution)/shard_map/broadcast_in_dim | solution.py:149
  142.2 4.2 %reshape.431 = bf16[36,68,384]{2,1,0:T(8,128)(2,1)S(1)} reshape(bf16[36,34,2,384]{3,2,1,0:T(2,128)(2,1)} %broadcast_in_dim.42) | data formatting | bytes 3760128 | tf_op jit(solution)/shard_map/reshape | solution.py:149
  147.3 3.6 %fusion.100 = (bf16[1,32,64,384]{3,2,1,0:T(8,128)(2,1)S(1)}, bf16[1,32,64,384]{3,2,1,0:T(8,128)(2,1)S(1)}, bf16[1,32,64,384]{3,2,1,0:T(8,128)(2,1)S(1)}, bf16[1,...) fusion(bf16[1,34,66,384]{3,2,1,0:T(8,128)(2,1)S(1)} %slice_bitc, ...), kind=kLoop, calls=%fused_computation.217 | loop fusion | bytes 28311552 | tf_op jit(solution)/shard_map/slice | solution.py:29
  158.0 2.1 %reshape.433 = bf16[1,32,12288]{2,1,0:T(8,128)(2,1)} reshape(bf16[2048,192]{1,0:T(8,128)(2,1)S(1)} %copy.50) | data formatting | bytes 1572864 | tf_op jit(solution)/shard_map/reshape | solution.py:155
  (201 shorter events, 65.5 us)
Async XLA Ops:
  0.0 88.7 %copy-start = (bf16[432,384]{1,0:T(8,128)(2,1)S(1)}, bf16[432,384]{1,0:T(8,128)(2,1)}, u32[]{:S(2)}) copy-start(bf16[432,384]{1,0:T(8,128)(2,1)} %param.17) | copy-start | bytes 995332
  0.0 21.6 %copy-start.12 = (bf16[1,2,16,512]{3,2,1,0:T(8,128)(2,1)S(1)}, bf16[1,2,16,512]{3,2,1,0:T(8,128)(2,1)}, u32[]{:S(2)}) copy-start(bf16[1,2,16,512]{3,2,1,0:T(8,128)(2,1)} %param.15) | copy-start | bytes 98308
  20.0 32.0 %copy-start.9 = (bf16[1,2,16,12288]{3,2,1,0:T(8,128)(2,1)S(1)}, bf16[1,2,16,12288]{3,2,1,0:T(8,128)(2,1)}, u32[]{:S(2)}) copy-start(bf16[1,2,16,12288]{3,2,1,0:T(8,128)(2,1)} %param.16) | copy-start | bytes 2359300
  47.8 6.0 %collective-permute-start = (bf16[3,1,32,16]{3,2,1,0:T(8,128)(2,1)S(1)}, bf16[3,1,32,16]{3,2,1,0:T(8,128)(2,1)S(1)}, u32[]{:S(2)}, u32[]{:S(2)}) collective-permute-start(bf16[3,1,32,16]{3,2,1,0:T(8,128)(2,1)S(1)} %get-tuple-element.84), channel_id=1, source_target_pairs={{0,4},{1,5},{2,6},{3,7},{8,12},{9,13},{10,14},{11,15},{16,20},{17,... | collective-permute-start | bytes 9224 | tf_op jit(solution)/shard_map/ppermute | solution.py:16
  50.6 4.6 %collective-permute-start.1 = (bf16[3,1,32,16]{3,2,1,0:T(8,128)(2,1)S(1)}, bf16[3,1,32,16]{3,2,1,0:T(8,128)(2,1)S(1)}, u32[]{:S(2)}, u32[]{:S(2)}) collective-permute-start(bf16[3,1,32,16]{3,2,1,0:T(8,128)(2,1)S(1)} %get-tuple-element.85), channel_id=1, source_target_pairs={{4,0},{5,1},{6,2},{7,3},{12,8},{13,9},{14,10},{15,11},{20,16},{21,... | collective-permute-start | bytes 9224 | tf_op jit(solution)/shard_map/ppermute | solution.py:17
  56.2 9.9 %collective-permute-start.3 = (bf16[3,18,1,16]{3,2,1,0:T(2,128)(2,1)}, bf16[3,18,1,16]{3,2,1,0:T(2,128)(2,1)}, u32[]{:S(2)}, u32[]{:S(2)}) collective-permute-start(bf16[3,18,1,16]{3,2,1,0:T(2,128)(2,1)} %get-tuple-element.68), channel_id=1, source_target_pairs={{1,0},{2,1},{3,2},{5,4},{6,5},{7,6},{9,8},{10,9},{11,10},{13,12},{... | collective-permute-start | bytes 5192 | tf_op jit(solution)/shard_map/ppermute | solution.py:17
  59.7 8.7 %collective-permute-start.2 = (bf16[3,18,1,16]{3,2,1,0:T(2,128)(2,1)}, bf16[3,18,1,16]{3,2,1,0:T(2,128)(2,1)}, u32[]{:S(2)}, u32[]{:S(2)}) collective-permute-start(bf16[3,18,1,16]{3,2,1,0:T(2,128)(2,1)} %get-tuple-element.69), channel_id=1, source_target_pairs={{0,1},{1,2},{2,3},{4,5},{5,6},{6,7},{8,9},{9,10},{10,11},{12,13},{... | collective-permute-start | bytes 5192 | tf_op jit(solution)/shard_map/ppermute | solution.py:16
  70.8 2.2 %copy-start.10 = (bf16[512,16]{0,1:T(8,128)(2,1)S(1)}, bf16[512,16]{0,1:T(8,128)(2,1)}, u32[]{:S(2)}) copy-start(bf16[512,16]{0,1:T(8,128)(2,1)} %copy.41) | copy-start | bytes 49156
  70.8 2.8 %copy-start.11 = (bf16[512,16]{0,1:T(8,128)(2,1)S(1)}, bf16[512,16]{0,1:T(8,128)(2,1)}, u32[]{:S(2)}) copy-start(bf16[512,16]{0,1:T(8,128)(2,1)} %concatenate.149) | copy-start | bytes 49156
  71.3 17.4 %copy-start.16 = (f32[384]{0:T(512)S(1)}, f32[384]{0:T(512)}, u32[]{:S(2)}) copy-start(f32[384]{0:T(512)} %param.18) | copy-start | bytes 4612
  72.6 17.8 %copy-start.13 = (f32[384]{0:T(512)S(1)}, f32[384]{0:T(512)}, u32[]{:S(2)}) copy-start(f32[384]{0:T(512)} %param.19) | copy-start | bytes 4612
  88.7 18.6 %slice-start = ((s8[7962624]{0:T(1024)(128)(4,1)}), s8[4194304]{0:T(1024)(128)(4,1)S(1)}, s32[]{:S(2)}) async-start(s8[7962624]{0:T(1024)(128)(4,1)} %bitcast.186), calls=%async_computation | async-start | bytes 8388608
  90.8 4.9 %collective-permute-start.4 = (bf16[3,1,32,384]{3,2,1,0:T(8,128)(2,1)S(1)}, bf16[3,1,32,384]{3,2,1,0:T(8,128)(2,1)S(1)}, u32[]{:S(2)}, u32[]{:S(2)}) collective-permute-start(bf16[3,1,32,384]{3,2,1,0:T(8,128)(2,1)S(1)} %get-tuple-element.45), channel_id=1, source_target_pairs={{0,4},{1,5},{2,6},{3,7},{8,12},{9,13},{10,14},{11,15},{16,20},{17,... | collective-permute-start | bytes 221192 | tf_op jit(solution)/shard_map/ppermute | solution.py:16
  93.1 5.6 %collective-permute-start.5 = (bf16[3,1,32,384]{3,2,1,0:T(8,128)(2,1)S(1)}, bf16[3,1,32,384]{3,2,1,0:T(8,128)(2,1)S(1)}, u32[]{:S(2)}, u32[]{:S(2)}) collective-permute-start(bf16[3,1,32,384]{3,2,1,0:T(8,128)(2,1)S(1)} %get-tuple-element.46), channel_id=1, source_target_pairs={{4,0},{5,1},{6,2},{7,3},{12,8},{13,9},{14,10},{15,11},{20,16},{21,... | collective-permute-start | bytes 221192 | tf_op jit(solution)/shard_map/ppermute | solution.py:17
  95.7 11.6 %slice-start.1 = ((s8[7962624]{0:T(1024)(128)(4,1)}), s8[3768320]{0:T(1024)(128)(4,1)S(1)}, s32[]{:S(2)}) async-start(s8[7962624]{0:T(1024)(128)(4,1)} %bitcast.186), calls=%async_computation.1 | async-start | bytes 7536640
  100.5 9.7 %collective-permute-start.6 = (bf16[3,18,1,384]{3,2,1,0:T(2,128)(2,1)S(1)}, bf16[3,18,1,384]{3,2,1,0:T(2,128)(2,1)S(1)}, u32[]{:S(2)}, u32[]{:S(2)}) collective-permute-start(bf16[3,18,1,384]{3,2,1,0:T(2,128)(2,1)S(1)} %get-tuple-element.34), channel_id=1, source_target_pairs={{0,1},{1,2},{2,3},{4,5},{5,6},{6,7},{8,9},{9,10},{10,11},{12,13},{... | collective-permute-start | bytes 124424 | tf_op jit(solution)/shard_map/ppermute | solution.py:16
  103.8 6.4 %collective-permute-start.7 = (bf16[3,18,1,384]{3,2,1,0:T(2,128)(2,1)S(1)}, bf16[3,18,1,384]{3,2,1,0:T(2,128)(2,1)S(1)}, u32[]{:S(2)}, u32[]{:S(2)}) collective-permute-start(bf16[3,18,1,384]{3,2,1,0:T(2,128)(2,1)S(1)} %get-tuple-element.35), channel_id=1, source_target_pairs={{1,0},{2,1},{3,2},{5,4},{6,5},{7,6},{9,8},{10,9},{11,10},{13,12},{... | collective-permute-start | bytes 124424 | tf_op jit(solution)/shard_map/ppermute | solution.py:17
  121.5 1.2 copy-start.3
  123.3 2.7 %collective-permute-start.8 = (bf16[1,32,384]{2,1,0:T(8,128)(2,1)S(1)}, bf16[1,32,384]{2,1,0:T(8,128)(2,1)S(1)}, u32[]{:S(2)}, u32[]{:S(2)}) collective-permute-start(bf16[1,32,384]{2,1,0:T(8,128)(2,1)S(1)} %get-tuple-element.76), channel_id=1, source_target_pairs={{0,4},{1,5},{2,6},{3,7},{8,12},{9,13},{10,14},{11,15},{16,20},{17,... | collective-permute-start | bytes 73736 | tf_op jit(solution)/shard_map/ppermute | solution.py:16
  124.8 4.6 %collective-permute-start.9 = (bf16[1,32,384]{2,1,0:T(8,128)(2,1)S(1)}, bf16[1,32,384]{2,1,0:T(8,128)(2,1)S(1)}, u32[]{:S(2)}, u32[]{:S(2)}) collective-permute-start(bf16[1,32,384]{2,1,0:T(8,128)(2,1)S(1)} %get-tuple-element.77), channel_id=1, source_target_pairs={{4,0},{5,1},{6,2},{7,3},{12,8},{13,9},{14,10},{15,11},{20,16},{21,... | collective-permute-start | bytes 73736 | tf_op jit(solution)/shard_map/ppermute | solution.py:17
  129.4 7.8 %collective-permute-start.10 = (bf16[18,1,384]{2,1,0:T(2,128)(2,1)S(1)}, bf16[18,1,384]{2,1,0:T(2,128)(2,1)S(1)}, u32[]{:S(2)}, u32[]{:S(2)}) collective-permute-start(bf16[18,1,384]{2,1,0:T(2,128)(2,1)S(1)} %get-tuple-element.48), channel_id=1, source_target_pairs={{0,1},{1,2},{2,3},{4,5},{5,6},{6,7},{8,9},{9,10},{10,11},{12,13},{... | collective-permute-start | bytes 41480 | tf_op jit(solution)/shard_map/ppermute | solution.py:16
  134.5 5.2 %collective-permute-start.11 = (bf16[18,1,384]{2,1,0:T(2,128)(2,1)S(1)}, bf16[18,1,384]{2,1,0:T(2,128)(2,1)S(1)}, u32[]{:S(2)}, u32[]{:S(2)}) collective-permute-start(bf16[18,1,384]{2,1,0:T(2,128)(2,1)S(1)} %get-tuple-element.49), channel_id=1, source_target_pairs={{1,0},{2,1},{3,2},{5,4},{6,5},{7,6},{9,8},{10,9},{11,10},{13,12},{... | collective-permute-start | bytes 41480 | tf_op jit(solution)/shard_map/ppermute | solution.py:17
  147.3 3.6 %copy-start.8 = (bf16[3456,192]{0,1:T(8,128)(2,1)S(1)}, bf16[3456,192]{0,1:T(8,128)(2,1)}, u32[]{:S(2)}) copy-start(bf16[3456,192]{0,1:T(8,128)(2,1)} %param.22) | copy-start | bytes 3981316
  156.8 3.3 %copy-start.1 = (bf16[432,384]{1,0:T(8,128)(2,1)S(1)}, bf16[432,384]{1,0:T(8,128)(2,1)}, u32[]{:S(2)}) copy-start(bf16[432,384]{1,0:T(8,128)(2,1)} %param.17) | copy-start | bytes 995332
  (7 other events, 7.2 us)
where the time goes:
time: 161 us; the launch traced here: 160 us
  local copies, waits for them, and re-layouts  71.1 us (44%)
  starting transfers between devices  29.1 us (18%)
  matrix products  24.5 us (15%)
  blocking collectives  11.2 us (7%)
  other arithmetic  11.1 us (7%)
  waiting for transfers between devices  10.2 us (6%)
  between operations  2.86 us (2%)
    scatter x1, local copies, waits for them, and re-layouts, per_device(): jnp.zeros((tile_cells, latent_width), jnp.bfloat16).at[target]  24.5 us
    dot_general x36, matrix products, tap_sum(): jnp.dot(window, weight[tap_index * channels:(tap_index + 1) * channels],...  22.8 us
    ppermute x6, starting transfers between devices, padded_2(): before = lax.ppermute(last, axis, up)  17.4 us
    unnamed x65, local copies, waits for them, and re-layouts  16.8 us
    ppermute x6, starting transfers between devices, padded_2(): after = lax.ppermute(leading, axis, down)  11.7 us
    all_gather x1, blocking collectives, per_device(): lax.all_gather(latent_shards, ('ty', 'tx'), axis=1, tiled=True)  11.2 us
    ppermute x6, waiting for transfers between devices, padded_2(): after = lax.ppermute(leading, axis, down)  10.2 us
    concatenate x28, local copies, waits for them, and re-layouts, unfold_taps(): joined = jnp.concatenate(pieces, axis=-1)  6.48 us
  transfers between devices with their start and end apart: 12, of which 4 were waited for; matrix products, arithmetic and copies ran while one was open for 9% of the time, Pallas kernels for 0%

commit v1 on v0

v1 whole, which is shorter than its diff:
```python
import functools

import jax
import jax.numpy as jnp
from jax import lax
from jax.experimental import pallas as pl
from jax.experimental.pallas import tpu as pltpu
from jax.sharding import PartitionSpec as P

EPS = 1e-06
F32 = jnp.float32
BF16 = jnp.bfloat16


def padded_2(value, sides, width):
    for axis, dim in sides:
        size, length = (lax.axis_size(axis), value.shape[dim])
        up = [(i, (i + 1) % size) for i in range(size - 1)]
        down = [(j, i) for i, j in up]
        wide = width[dim]
        last = lax.slice_in_dim(value, length - wide, length, axis=dim)
        leading = lax.slice_in_dim(value, 0, wide, axis=dim)
        before = lax.ppermute(last, axis, up)
        after = lax.ppermute(leading, axis, down)
        value = jnp.concatenate([before, value, after], axis=dim)
    return value


SLOT = 24
HIGH = 32


def compute_kernel(
    shards,
    starts_ref,
    dims_ref,
    tok_ref,
    lat_ref,
    feat_ref,
    in_w_ref,
    in_b_ref,
    gain_ref,
    res_w_ref,
    res_b_ref,
    up_w_ref,
    up_b_ref,
    out_ref,
    weights,
    toks,
    rows_s,
    lat_s,
    band,
    lat_lhs,
    upw,
    first_raw,
    stage,
    values,
    lhs,
    acc,
    grown,
    upacc,
    out_s,
    sems,
):
    channels = in_b_ref.shape[1]
    lanes = 3 * channels
    copies = []
    for f in range(3):
        for a in range(3):
            copy = pltpu.make_async_copy(
                res_w_ref.at[pl.ds((f * 3 + a) * lanes, lanes), :],
                weights.at[f, :, pl.ds(a * channels, channels)],
                sems.at[f * 3 + a],
            )
            copy.start()
            copies.append(copy)
    row0 = lax.axis_index("ty") * 16
    col0 = lax.axis_index("tx") * 32
    height = dims_ref[0, 0]
    breadth = dims_ref[0, 1]

    band[...] = jnp.zeros_like(band)
    for fa in range(9):
        block = in_w_ref[fa * 48 : fa * 48 + 48, :]
        for i in range(6):
            band[fa * 128 + i * 16 : fa * 128 + i * 16 + 48, i * channels : (i + 1) * channels] = (
                block
            )

    halves = (((0,), (1, 2)), ((0, 1), (2,)))

    def up_sum(pr, ar, pc, ac):
        total = None
        for a in halves[pr][ar]:
            for b in halves[pc][ac]:
                at = (a * 3 + b) * channels
                part = up_w_ref[at : at + channels, :].astype(F32)
                total = part if total is None else total + part
        return total

    for pr in range(2):
        for ar in range(2):
            near = jnp.concatenate([up_sum(pr, ar, 0, 1), up_sum(pr, ar, 1, 0)], axis=1)
            far = jnp.concatenate([up_sum(pr, ar, 0, 0), up_sum(pr, ar, 1, 1)], axis=1)
            upw[pr, ar * channels : (ar + 1) * channels, 0:channels] = near.astype(BF16)
            upw[pr, ar * channels : (ar + 1) * channels, channels : 2 * channels] = far.astype(
                BF16
            )

    token_rows = tok_ref.shape[1]
    for j in range(shards):
        toks[j] = jnp.zeros_like(toks[j])
        toks[j, 8 : 8 + token_rows, :] = tok_ref[j].astype(F32)
    lane = lax.broadcasted_iota(jnp.int32, (8, 128), 1)
    token = lax.broadcasted_iota(jnp.int32, (8, 128), 0) * 8 + lane // 16
    rows_s[...] = jnp.zeros_like(rows_s)

    def one_row(slab_row, carry):
        row = row0 + slab_row - 8
        first = row * breadth + col0 - 3
        col = token + (col0 - 3)
        place = token + first
        live = (col >= 0) & (col < breadth) & (row >= 0) & (row < height)
        picked = jnp.zeros((8, 128), F32)
        for j in range(shards):
            begin = starts_ref[0, j]
            end = starts_ref[0, j + 1]
            slot = jnp.clip(first - begin + 64, 0, (token_rows + 8) * 8)
            read = toks[j, pl.ds(slot >> 3, 8), :]
            shift = (slot & 7) * 16
            turned = pltpu.roll(read, lax.rem(128 - shift, 128), axis=1)
            after = pltpu.roll(turned, 7, axis=0)
            value = jnp.where(lane < 128 - shift, turned, after)
            picked = jnp.where((place >= begin) & (place < end), value, picked)
        rows_s[pl.ds(pl.multiple_of(slab_row * 8, 8), 8), :] = jnp.where(live, picked, 0.0)
        return carry

    lax.fori_loop(5, 27, one_row, 0)
    lat_lane = lax.broadcasted_iota(jnp.int32, (HIGH, 640), 1)
    lat_col = lat_lane // 16 + (col0 - 3)
    lat_row = lax.broadcasted_iota(jnp.int32, (HIGH, 640), 0) + (row0 - 8)
    lat_keep = (lat_row >= 0) & (lat_row < height) & (lat_col >= 0) & (lat_col < breadth)
    for f in range(2):
        lat_s[f] = jnp.where(lat_keep, lat_ref[f].astype(F32), 0.0)
    for g in range(5):
        lat_s[2, :, g * 128 : (g + 1) * 128] = rows_s[pl.ds(g, HIGH, stride=8), :]

    for f in range(3):
        frame = lat_s[f]
        for a in range(3):
            moved = frame if a == 1 else pltpu.roll(frame, 1 if a == 0 else HIGH - 1, axis=0)
            for g in range(6):
                lat_lhs[g * HIGH : (g + 1) * HIGH, (f * 3 + a) * 128 : (f * 3 + a + 1) * 128] = (
                    moved[:, g * 96 : g * 96 + 128].astype(BF16)
                )
    first_raw[...] = jnp.dot(lat_lhs[...], band[...], preferred_element_type=F32)

    slab_row = lax.broadcasted_iota(jnp.int32, (HIGH, channels), 0)
    row_ok = (slab_row + (row0 - 8) >= 0) & (slab_row + (row0 - 8) < height)
    row_ok_near = row_ok & (slab_row >= 6) & (slab_row < 26)
    eighth = lax.broadcasted_iota(jnp.int32, (8, channels), 0)

    def put_slab(dest, c, slab, before):
        head = slab[0:8] if before is None else jnp.where(eighth < 4, before, slab[0:8])
        dest[c * SLOT : c * SLOT + 8, :] = head
        dest[c * SLOT + 8 : c * SLOT + 24, :] = slab[8:24]
        return slab[24:32]

    def finish_lhs(f):
        for b in range(3):
            lhs[f, :, b * channels : (b + 1) * channels] = stage[
                b * SLOT : b * SLOT + lhs.shape[1], :
            ].astype(BF16)

    def col_ok(c):
        col = col0 - 2 + c
        return (col >= 0) & (col < breadth)

    tail = jnp.zeros((8, channels), F32)
    stage[36 * SLOT + 8 :, :] = jnp.zeros((stage.shape[0] - 36 * SLOT - 8, channels), F32)
    for f in range(2):
        before = tail
        for c in range(36):
            slab = feat_ref[f, :, c * channels : (c + 1) * channels].astype(F32)
            slab = jnp.where(row_ok_near & col_ok(c), slab, 0.0)
            before = put_slab(stage, c, slab, before)
        stage[36 * SLOT : 36 * SLOT + 8, :] = before
        finish_lhs(f)
    in_b = in_b_ref[...]
    gain = gain_ref[...]
    before = tail
    before_values = tail
    for c in range(36):
        g, i = c // 6, c % 6
        raw = first_raw[g * HIGH : (g + 1) * HIGH, i * channels : (i + 1) * channels]
        value = (raw + in_b).astype(BF16).astype(F32)
        power = jnp.mean(value * value, axis=1, keepdims=True)
        normed = value * lax.rsqrt(power + EPS) * gain
        hidden = normed / (1.0 + jnp.exp(-normed))
        hidden = jnp.where(row_ok_near & col_ok(c), hidden, 0.0)
        before = put_slab(stage, c, hidden, before)
        before_values = put_slab(values, c, value, before_values)
    stage[36 * SLOT : 36 * SLOT + 8, :] = before
    values[36 * SLOT : 36 * SLOT + 8, :] = before_values
    finish_lhs(2)

    for copy in copies:
        copy.wait()

    def frame_dot(f, carry):
        part = jnp.dot(lhs[f], weights[f], preferred_element_type=F32)

        @pl.when(f == 0)
        def _():
            acc[...] = part

        @pl.when(f > 0)
        def _():
            acc[...] += part

        return carry

    lax.fori_loop(0, 3, frame_dot, 0)

    res_b = res_b_ref[...]
    for c in range(34):
        rows = pl.ds(c * SLOT, HIGH)
        slab = acc[rows, channels : 2 * channels]
        slab += pltpu.roll(acc[rows, 0:channels], 1, axis=0)
        slab += pltpu.roll(acc[rows, 2 * channels :], HIGH - 1, axis=0)
        slab += values[pl.ds((c + 1) * SLOT, HIGH), :]
        slab = jnp.where(row_ok & col_ok(c + 1), slab + res_b, 0.0)
        at = c * 16
        grown[at : at + 16, 0:channels] = pltpu.roll(slab, 1, axis=0)[8:24].astype(BF16)
        grown[at : at + 16, channels : 2 * channels] = slab[8:24].astype(BF16)
        grown[at : at + 16, 2 * channels :] = pltpu.roll(slab, HIGH - 1, axis=0)[8:24].astype(BF16)

    up_b = jnp.concatenate([up_b_ref[...], up_b_ref[...]], axis=1)
    left = lax.broadcasted_iota(jnp.int32, (16, channels), 1) < channels // 2
    own_row = row_ok[8:24]
    for pr in range(2):
        upacc[...] = jnp.dot(
            grown[:, pr * channels : (pr + 2) * channels], upw[pr], preferred_element_type=F32
        )
        for j in range(32):
            centre = upacc[(j + 1) * 16 : (j + 2) * 16, 0:channels]
            west = upacc[j * 16 : (j + 1) * 16, channels:]
            east = upacc[(j + 2) * 16 : (j + 3) * 16, channels:]
            slab = centre + jnp.where(left, west, east) + up_b
            slab = jnp.where(own_row & col_ok(j + 2), slab, 0.0)
            for k in range(channels // 128):
                out_s[j * 3 + k, pl.ds(pr, 16, stride=2), :] = slab[:, k * 128 : (k + 1) * 128]
    for j in range(32 * 3):
        out_ref[:, j * 128 : (j + 1) * 128] = out_s[j].astype(BF16)


def compute(shards, starts, dims, tok, lat, feat, weights):
    in_w, in_b, gain, res_w, res_b, up_w, up_b = weights
    channels = in_b.shape[0]
    out_width = up_b.shape[0]
    cells = 34 * SLOT + 16
    vmem = pl.BlockSpec(memory_space=pltpu.VMEM)
    smem = pl.BlockSpec(memory_space=pltpu.SMEM)
    return pl.pallas_call(
        functools.partial(compute_kernel, shards),
        out_shape=jax.ShapeDtypeStruct((32, 64 * out_width), BF16),
        in_specs=[smem, smem, vmem, vmem, vmem, vmem, vmem, vmem]
        + [pl.BlockSpec(memory_space=pl.ANY), vmem, vmem, vmem],
        out_specs=vmem,
        scratch_shapes=[
            pltpu.VMEM((3, 3 * channels, 3 * channels), BF16),
            pltpu.VMEM((shards, (tok.shape[1] + 16 + 15) // 8 * 8, 128), F32),
            pltpu.VMEM((HIGH * 8, 128), F32),
            pltpu.VMEM((3, HIGH, 640), F32),
            pltpu.VMEM((9 * 128, 6 * channels), BF16),
            pltpu.VMEM((6 * HIGH, 9 * 128), BF16),
            pltpu.VMEM((2, 2 * channels, 2 * channels), BF16),
            pltpu.VMEM((6 * HIGH, 6 * channels), F32),
            pltpu.VMEM((cells + 2 * SLOT, channels), F32),
            pltpu.VMEM((cells + 2 * SLOT, channels), F32),
            pltpu.VMEM((3, cells, 3 * channels), BF16),
            pltpu.VMEM((cells, 3 * channels), F32),
            pltpu.VMEM((34 * 16, 3 * channels), BF16),
            pltpu.VMEM((34 * 16, 2 * channels), F32),
            pltpu.VMEM((32 * 3, 32, 128), F32),
            pltpu.SemaphoreType.DMA((9,)),
        ],
        compiler_params=pltpu.CompilerParams(vmem_limit_bytes=56 * 1024 * 1024),
        cost_estimate=pl.CostEstimate(
            flops=9_000_000_000, bytes_accessed=13_000_000, transcendentals=400_000
        ),
    )(
        starts,
        dims,
        tok,
        lat,
        feat,
        in_w,
        in_b.reshape(1, -1),
        gain.reshape(1, -1),
        res_w,
        res_b.reshape(1, -1),
        up_w,
        up_b.reshape(1, -1),
    )


def per_device(
    latent_shards,
    shard_starts,
    frame_dims,
    latent_cache,
    feature_cache,
    *weights,
):
    channels = weights[1].shape[0]
    latent_width = weights[0].shape[0] // 27
    shard_count = lax.axis_size("ty") * lax.axis_size("tx")
    tok = lax.all_gather(latent_shards, ("ty", "tx"), axis=1, tiled=True)
    tok = tok.reshape(shard_count, -1, 128)
    sides = (("ty", 1), ("tx", 2))
    lat = padded_2(latent_cache[0], sides, {1: 3, 2: 3 * latent_width})
    lat = jnp.pad(lat, ((0, 0), (5, 5), (0, 32)))
    feat = padded_2(feature_cache[0], sides, {1: 2, 2: 2 * channels})
    feat = jnp.pad(feat, ((0, 0), (6, 6), (0, 0)))
    out = compute(shard_count, shard_starts, frame_dims, tok, lat, feat, weights)
    return out[None]


def solution(mesh):
    return jax.shard_map(
        per_device,
        mesh=mesh,
        in_specs=(
            P("vid", ("ty", "tx")),
            P("vid", None),
            P("vid", None),
            P("vid", None, "ty", "tx"),
            P("vid", None, "ty", "tx"),
            P(),
            P(),
            P(),
            P(),
            P(),
            P(),
            P(),
        ),
        out_specs=P("vid", "ty", "tx"),
        check_vma=False,
    )
```

time: 161 us -> 70.1 us (0.44)
  local copies, waits for them, and re-layouts: 71.1 us -> 8.84 us
  matrix products: 24.5 us -> 0 us
  Pallas kernels: 0 us -> 20.6 us
  starting transfers between devices: 29.1 us -> 20.9 us
  other arithmetic: 11.1 us -> 3.74 us
  waiting for transfers between devices: 10.2 us -> 3 us
  between operations: 2.86 us -> 0.14 us
    dot_general x37 -> x0, matrix products: 24.5 us -> none  [the longest x36 22.8 us: tap_sum(): jnp.dot(window, weight[tap_index * channels:(tap_index + 1) * channels],...]
    scatter x1 -> x0, local copies, waits for them, and re-layouts: 24.5 us -> none  [per_device(): jnp.zeros((tile_cells, latent_width), jnp.bfloat16).at[target]]
    pallas_call x0 -> x1, Pallas kernels: none -> 20.6 us  [compute(): pl.pallas_call(functools.partial(compute_kernel, shards), out_shape=jax.S...]
    unnamed x65 -> x7, local copies, waits for them, and re-layouts: 16.8 us -> 2.19 us
    ppermute x6 -> x4, waiting for transfers between devices: 10.2 us -> 2.99 us  [padded_2(): after = lax.ppermute(leading, axis, down)]
    concatenate x29 -> x0, local copies, waits for them, and re-layouts: 6.7 us -> none  [the longest x28 6.48 us: unfold_taps(): joined = jnp.concatenate(pieces, axis=-1)]
    slice x26 -> x2, local copies, waits for them, and re-layouts: 8.67 us -> 2.12 us  [padded_2(): last = lax.slice_in_dim(value, length - wide, length, axis=dim)]
    ppermute x6 -> x4, starting transfers between devices: 11.7 us -> 6.43 us  [padded_2(): after = lax.ppermute(leading, axis, down)]
  transfers between devices with their start and end apart: 12 -> 8, of which waited for: 4 -> 1; matrix products, arithmetic and copies ran while one was open for 9% -> 14% of each run, Pallas kernels for 0% -> 0%
where the time goes in v1:
time: 70.1 us; the launch traced here: 69.6 us
  starting transfers between devices  20.9 us (30%)
  Pallas kernels  20.6 us (29%)
  blocking collectives  12.3 us (18%)
  local copies, waits for them, and re-layouts  8.84 us (13%)
  other arithmetic  3.74 us (5%)
  waiting for transfers between devices  3 us (4%)
    pallas_call x1, Pallas kernels, compute(): pl.pallas_call(functools.partial(compute_kernel, shards), out_shape=jax.S...  20.6 us
    ppermute x4, starting transfers between devices, padded_2(): before = lax.ppermute(last, axis, up)  14.5 us
    all_gather x1, blocking collectives, per_device(): tok = lax.all_gather(latent_shards, ('ty', 'tx'), axis=1, tiled=True)  12.3 us
    ppermute x4, starting transfers between devices, padded_2(): after = lax.ppermute(leading, axis, down)  6.43 us
    ppermute x4, waiting for transfers between devices, padded_2(): after = lax.ppermute(leading, axis, down)  2.99 us
    concatenate x2, other arithmetic, padded_2(): value = jnp.concatenate([before, value, after], axis=dim)  2.41 us
    unnamed x7, local copies, waits for them, and re-layouts  2.19 us
    slice x2, local copies, waits for them, and re-layouts, padded_2(): last = lax.slice_in_dim(value, length - wide, length, axis=dim)  2.12 us
  transfers between devices with their start and end apart: 8, of which 1 were waited for; matrix products, arithmetic and copies ran while one was open for 14% of the time, Pallas kernels for 0%

profile of v1, /device:TPU:1, one launch (start us, length us, event | category | flops | bytes accessed | tf_op | source)
XLA Modules:
  0.0 69.6 jit_solution(1189718251731130521)
XLA Ops:
  0.0 0.8 %fusion.17 = (bf16[2,3,512]{2,1,0:T(4,128)(2,1)S(1)}, bf16[2,3,512]{2,1,0:T(4,128)(2,1)S(1)}) fusion(bf16[2,16,512]{2,1,0:T(8,128)(2,1)} %bitcast.7), kind=kLoop, calls=%fused_computation.32 | loop fusion | bytes 24576 | tf_op jit(solution)/shard_map/slice | solution.py:21
  0.9 4.0 %collective-permute-start = (bf16[2,3,512]{2,1,0:T(4,128)(2,1)S(1)}, bf16[2,3,512]{2,1,0:T(4,128)(2,1)S(1)}, u32[]{:S(2)}, u32[]{:S(2)}) collective-permute-start(bf16[2,3,512]{2,1,0:T(4,128)(2,1)S(1)} %get-tuple-element.11), channel_id=1, source_target_pairs={{0,4},{1,5},{2,6},{3,7},{8,12},{9,13},{10,14},{11,15},{16,20},{17,... | collective-permute-start | bytes 18440 | tf_op jit(solution)/shard_map/ppermute | solution.py:23
  4.8 1.3 %collective-permute-start.1 = (bf16[2,3,512]{2,1,0:T(4,128)(2,1)S(1)}, bf16[2,3,512]{2,1,0:T(4,128)(2,1)S(1)}, u32[]{:S(2)}, u32[]{:S(2)}) collective-permute-start(bf16[2,3,512]{2,1,0:T(4,128)(2,1)S(1)} %get-tuple-element.12), channel_id=1, source_target_pairs={{4,0},{5,1},{6,2},{7,3},{12,8},{13,9},{14,10},{15,11},{20,16},{21,... | collective-permute-start | bytes 18440 | tf_op jit(solution)/shard_map/ppermute | solution.py:24
  6.1 1.3 %fusion.16 = (bf16[2,2,12288]{2,1,0:T(2,128)(2,1)S(1)}, bf16[2,2,12288]{2,1,0:T(2,128)(2,1)S(1)}) fusion(bf16[2,16,12288]{2,1,0:T(8,128)(2,1)} %bitcast.4), kind=kLoop, calls=%fused_computation.31 | loop fusion | bytes 393216 | tf_op jit(solution)/shard_map/slice | solution.py:21
  7.4 4.0 %collective-permute-start.4 = (bf16[2,2,12288]{2,1,0:T(2,128)(2,1)S(1)}, bf16[2,2,12288]{2,1,0:T(2,128)(2,1)S(1)}, u32[]{:S(2)}, u32[]{:S(2)}) collective-permute-start(bf16[2,2,12288]{2,1,0:T(2,128)(2,1)S(1)} %get-tuple-element.7), channel_id=1, source_target_pairs={{0,4},{1,5},{2,6},{3,7},{8,12},{9,13},{10,14},{11,15},{16,20},{17,... | collective-permute-start | bytes 294920 | tf_op jit(solution)/shard_map/ppermute | solution.py:23
  11.4 1.3 %collective-permute-start.5 = (bf16[2,2,12288]{2,1,0:T(2,128)(2,1)S(1)}, bf16[2,2,12288]{2,1,0:T(2,128)(2,1)S(1)}, u32[]{:S(2)}, u32[]{:S(2)}) collective-permute-start(bf16[2,2,12288]{2,1,0:T(2,128)(2,1)S(1)} %get-tuple-element.8), channel_id=1, source_target_pairs={{4,0},{5,1},{6,2},{7,3},{12,8},{13,9},{14,10},{15,11},{20,16},{21,... | collective-permute-start | bytes 294920 | tf_op jit(solution)/shard_map/ppermute | solution.py:24
  12.7 12.3 %all_gather.3 = bf16[1,99328]{1,0:T(2,128)(2,1)S(1)} all-gather(bf16[1,12416]{1,0:T(2,128)(2,1)} %param.12), channel_id=1, replica_groups=mesh['vid'=4,'ty'=2,'tx'=4] {'ty','tx'}, dimensions={1}, use_global_device_ids=true | all-gather | bytes 223488 | tf_op jit(solution)/shard_map/all_gather | solution.py:319
  25.0 1.3 %reshape.16.in_b_ref = f32[1,384]{1,0:T(1,128)} reshape(f32[384]{0:T(512)} %param.18) | data formatting | bytes 3072 | tf_op jit(solution)/shard_map/reshape | solution.py:299
  26.3 1.3 %reshape.17.gain_ref = f32[1,384]{1,0:T(1,128)} reshape(f32[384]{0:T(512)} %param.19) | data formatting | bytes 3072 | tf_op jit(solution)/shard_map/reshape | solution.py:300
  27.6 1.3 %reshape.18.res_b_ref = f32[1,384]{1,0:T(1,128)} reshape(f32[384]{0:T(512)} %param.21) | data formatting | bytes 3072 | tf_op jit(solution)/shard_map/reshape | solution.py:302
  28.8 1.2 %reduce = bf16[99328]{0:T(1024)(128)(2,1)S(1)} reduce(bf16[1,99328]{1,0:T(2,128)(2,1)S(1)} %all_gather.3, bf16[]{:T(256)} %constant.12), dimensions={0}, to_apply=%all_gather.3.reduce_sub_computation | reduce | bytes 397314 | tf_op jit(solution)/shard_map/all_gather | solution.py:319
  30.0 0.0 copy-start
  30.0 0.8 %reshape.15.tok_ref = bf16[8,97,128]{2,1,0:T(8,128)(2,1)} reshape(bf16[99328]{0:T(1024)(128)(2,1)S(1)} %reduce) | data formatting | bytes 397312 | tf_op jit(solution)/shard_map/reshape | solution.py:320
  30.8 2.2 %copy.14.up_w_ref = bf16[3456,192]{1,0:T(8,128)(2,1)} copy(bf16[3456,192]{0,1:T(8,128)(2,1)S(1)} %copy-done.1) | data formatting | bytes 2654208 | tf_op args[10]
  33.0 0.1 pad_maximum_fusion.5
  33.1 2.9 %collective-permute-start.2 = (bf16[2,22,48]{2,1,0:T(8,128)(2,1)S(1)}, bf16[2,22,48]{2,1,0:T(8,128)(2,1)S(1)}, u32[]{:S(2)}, u32[]{:S(2)}) collective-permute-start(bf16[2,22,48]{2,1,0:T(8,128)(2,1)S(1)} %get-tuple-element.9), channel_id=1, source_target_pairs={{0,1},{1,2},{2,3},{4,5},{5,6},{6,7},{8,9},{9,10},{10,11},{12,13},{... | collective-permute-start | bytes 12680 | tf_op jit(solution)/shard_map/ppermute | solution.py:23
  36.0 1.9 %collective-permute-start.3 = (bf16[2,22,48]{2,1,0:T(8,128)(2,1)S(1)}, bf16[2,22,48]{2,1,0:T(8,128)(2,1)S(1)}, u32[]{:S(2)}, u32[]{:S(2)}) collective-permute-start(bf16[2,22,48]{2,1,0:T(8,128)(2,1)S(1)} %get-tuple-element.10), channel_id=1, source_target_pairs={{1,0},{2,1},{3,2},{5,4},{6,5},{7,6},{9,8},{10,9},{11,10},{13,12},{... | collective-permute-start | bytes 12680 | tf_op jit(solution)/shard_map/ppermute | solution.py:24
  37.9 0.1 pad_maximum_fusion.2
  38.0 3.6 %collective-permute-start.6 = (bf16[2,20,768]{2,1,0:T(8,128)(2,1)S(1)}, bf16[2,20,768]{2,1,0:T(8,128)(2,1)S(1)}, u32[]{:S(2)}, u32[]{:S(2)}) collective-permute-start(bf16[2,20,768]{2,1,0:T(8,128)(2,1)S(1)} %get-tuple-element.5), channel_id=1, source_target_pairs={{0,1},{1,2},{2,3},{4,5},{5,6},{6,7},{8,9},{9,10},{10,11},{12,13},{... | collective-permute-start | bytes 184328 | tf_op jit(solution)/shard_map/ppermute | solution.py:23
  41.6 1.9 %collective-permute-start.7 = (bf16[2,20,768]{2,1,0:T(8,128)(2,1)S(1)}, bf16[2,20,768]{2,1,0:T(8,128)(2,1)S(1)}, u32[]{:S(2)}, u32[]{:S(2)}) collective-permute-start(bf16[2,20,768]{2,1,0:T(8,128)(2,1)S(1)} %get-tuple-element.6), channel_id=1, source_target_pairs={{1,0},{2,1},{3,2},{5,4},{6,5},{7,6},{9,8},{10,9},{11,10},{13,12},{... | collective-permute-start | bytes 184328 | tf_op jit(solution)/shard_map/ppermute | solution.py:24
  43.6 0.7 %select_maximum_fusion.2.lat_ref = bf16[2,32,640]{2,1,0:T(8,128)(2,1)} fusion(bf16[2,22,48]{2,1,0:T(8,128)(2,1)S(1)} %collective-permute-done.3, bf16[2,22,48]{2,1,0:T(8,128)(2,1)S(1)} %collective-permute-done.2, bf16[2,3,512]{2,1,0:T(4,128)(2,1)S(1)} %collective-permute-done.1, bf16[2,16,512]{2,1,0:T(8,128)(2,1)S(1)} %bitcast.9, ...), kind=kLoop, calls=%fused_computation.15 | loop fusion | flops 1024000 | bytes 135424 | tf_op jit(solution)/shard_map/concatenate | solution.py:25
  44.3 3.0 %collective-permute-done.7 = bf16[2,20,768]{2,1,0:T(8,128)(2,1)S(1)} collective-permute-done((bf16[2,20,768]{2,1,0:T(8,128)(2,1)S(1)}, bf16[2,20,768]{2,1,0:T(8,128)(2,1)S(1)}, u32[]{:S(2)}, u32[]{:S(2)}) %collective-permute-start.7) | collective-permute-done | bytes 61472 | tf_op jit(solution)/shard_map/ppermute | solution.py:24
  47.3 1.7 %select_maximum_fusion.feat_ref = bf16[2,32,13824]{2,1,0:T(8,128)(2,1)} fusion(bf16[2,20,768]{2,1,0:T(8,128)(2,1)S(1)} %collective-permute-done.7, bf16[2,20,768]{2,1,0:T(8,128)(2,1)S(1)} %collective-permute-done.6, bf16[2,2,12288]{2,1,0:T(2,128)(2,1)S(1)} %collective-permute-done.5, bf16[2,16,12288]{2,1,0:T(8,128)(2,1)S(1)} %bitcast.6, ...), kind=kLoop, calls=%fused_computation.3 | loop fusion | flops 15925248 | bytes 2875392 | tf_op jit(solution)/shard_map/concatenate | solution.py:25
  49.0 20.6 %shard_map.118 = bf16[32,12288]{1,0:T(8,128)(2,1)} custom-call(s32[1,9]{1,0:T(1,128)} %starts_ref.1, s32[1,2]{1,0:T(1,128)} %dims_ref.1, bf16[8,97,128]{2,1,0:T(8,128)(2,1)} %reshape.15.tok_ref, bf16[2,32,640]{2,1,0:T(8,128)(2,1)} %select_maximum_fusion.2.lat_ref, bf16[2,32,13824]{2,1,0:T(8,128)(2,1)} %select_maximum_fusion.feat_ref, ...), custom_call_target="tpu_custom_call" | custom-call | flops 8999999488 | bytes 13000000 | tf_op jit(solution)/shard_map/pallas_call | solution.py:264
  (12 shorter events, 0.0 us)
Async XLA Ops:
  0.0 30.8 %copy-start.1 = (bf16[3456,192]{0,1:T(8,128)(2,1)S(1)}, bf16[3456,192]{0,1:T(8,128)(2,1)}, u32[]{:S(2)}) copy-start(bf16[3456,192]{0,1:T(8,128)(2,1)} %param.22) | copy-start | bytes 3981316
  0.9 32.1 %collective-permute-start = (bf16[2,3,512]{2,1,0:T(4,128)(2,1)S(1)}, bf16[2,3,512]{2,1,0:T(4,128)(2,1)S(1)}, u32[]{:S(2)}, u32[]{:S(2)}) collective-permute-start(bf16[2,3,512]{2,1,0:T(4,128)(2,1)S(1)} %get-tuple-element.11), channel_id=1, source_target_pairs={{0,4},{1,5},{2,6},{3,7},{8,12},{9,13},{10,14},{11,15},{16,20},{17,... | collective-permute-start | bytes 18440 | tf_op jit(solution)/shard_map/ppermute | solution.py:23
  4.8 28.1 %collective-permute-start.1 = (bf16[2,3,512]{2,1,0:T(4,128)(2,1)S(1)}, bf16[2,3,512]{2,1,0:T(4,128)(2,1)S(1)}, u32[]{:S(2)}, u32[]{:S(2)}) collective-permute-start(bf16[2,3,512]{2,1,0:T(4,128)(2,1)S(1)} %get-tuple-element.12), channel_id=1, source_target_pairs={{4,0},{5,1},{6,2},{7,3},{12,8},{13,9},{14,10},{15,11},{20,16},{21,... | collective-permute-start | bytes 18440 | tf_op jit(solution)/shard_map/ppermute | solution.py:24
  7.4 30.5 %collective-permute-start.4 = (bf16[2,2,12288]{2,1,0:T(2,128)(2,1)S(1)}, bf16[2,2,12288]{2,1,0:T(2,128)(2,1)S(1)}, u32[]{:S(2)}, u32[]{:S(2)}) collective-permute-start(bf16[2,2,12288]{2,1,0:T(2,128)(2,1)S(1)} %get-tuple-element.7), channel_id=1, source_target_pairs={{0,4},{1,5},{2,6},{3,7},{8,12},{9,13},{10,14},{11,15},{16,20},{17,... | collective-permute-start | bytes 294920 | tf_op jit(solution)/shard_map/ppermute | solution.py:23
  11.4 26.5 %collective-permute-start.5 = (bf16[2,2,12288]{2,1,0:T(2,128)(2,1)S(1)}, bf16[2,2,12288]{2,1,0:T(2,128)(2,1)S(1)}, u32[]{:S(2)}, u32[]{:S(2)}) collective-permute-start(bf16[2,2,12288]{2,1,0:T(2,128)(2,1)S(1)} %get-tuple-element.8), channel_id=1, source_target_pairs={{4,0},{5,1},{6,2},{7,3},{12,8},{13,9},{14,10},{15,11},{20,16},{21,... | collective-permute-start | bytes 294920 | tf_op jit(solution)/shard_map/ppermute | solution.py:24
  30.0 3.0 %copy-start.2 = (bf16[1,2,16,512]{3,2,1,0:T(8,128)(2,1)S(1)}, bf16[1,2,16,512]{3,2,1,0:T(8,128)(2,1)}, u32[]{:S(2)}) copy-start(bf16[1,2,16,512]{3,2,1,0:T(8,128)(2,1)} %param.15) | copy-start | bytes 98308
  30.0 7.9 %copy-start = (bf16[1,2,16,12288]{3,2,1,0:T(8,128)(2,1)S(1)}, bf16[1,2,16,12288]{3,2,1,0:T(8,128)(2,1)}, u32[]{:S(2)}) copy-start(bf16[1,2,16,12288]{3,2,1,0:T(8,128)(2,1)} %param.16) | copy-start | bytes 2359300
  33.1 10.5 %collective-permute-start.2 = (bf16[2,22,48]{2,1,0:T(8,128)(2,1)S(1)}, bf16[2,22,48]{2,1,0:T(8,128)(2,1)S(1)}, u32[]{:S(2)}, u32[]{:S(2)}) collective-permute-start(bf16[2,22,48]{2,1,0:T(8,128)(2,1)S(1)} %get-tuple-element.9), channel_id=1, source_target_pairs={{0,1},{1,2},{2,3},{4,5},{5,6},{6,7},{8,9},{9,10},{10,11},{12,13},{... | collective-permute-start | bytes 12680 | tf_op jit(solution)/shard_map/ppermute | solution.py:23
  36.0 7.6 %collective-permute-start.3 = (bf16[2,22,48]{2,1,0:T(8,128)(2,1)S(1)}, bf16[2,22,48]{2,1,0:T(8,128)(2,1)S(1)}, u32[]{:S(2)}, u32[]{:S(2)}) collective-permute-start(bf16[2,22,48]{2,1,0:T(8,128)(2,1)S(1)} %get-tuple-element.10), channel_id=1, source_target_pairs={{1,0},{2,1},{3,2},{5,4},{6,5},{7,6},{9,8},{10,9},{11,10},{13,12},{... | collective-permute-start | bytes 12680 | tf_op jit(solution)/shard_map/ppermute | solution.py:24
  38.0 6.3 %collective-permute-start.6 = (bf16[2,20,768]{2,1,0:T(8,128)(2,1)S(1)}, bf16[2,20,768]{2,1,0:T(8,128)(2,1)S(1)}, u32[]{:S(2)}, u32[]{:S(2)}) collective-permute-start(bf16[2,20,768]{2,1,0:T(8,128)(2,1)S(1)} %get-tuple-element.5), channel_id=1, source_target_pairs={{0,1},{1,2},{2,3},{4,5},{5,6},{6,7},{8,9},{9,10},{10,11},{12,13},{... | collective-permute-start | bytes 184328 | tf_op jit(solution)/shard_map/ppermute | solution.py:23
  41.6 5.7 %collective-permute-start.7 = (bf16[2,20,768]{2,1,0:T(8,128)(2,1)S(1)}, bf16[2,20,768]{2,1,0:T(8,128)(2,1)S(1)}, u32[]{:S(2)}, u32[]{:S(2)}) collective-permute-start(bf16[2,20,768]{2,1,0:T(8,128)(2,1)S(1)} %get-tuple-element.6), channel_id=1, source_target_pairs={{1,0},{2,1},{3,2},{5,4},{6,5},{7,6},{9,8},{10,9},{11,10},{13,12},{... | collective-permute-start | bytes 184328 | tf_op jit(solution)/shard_map/ppermute | solution.py:24

commit v2 on v1

--- a/solution.py
+++ b/solution.py
@@ -12,18 +12,7 @@
 BF16 = jnp.bfloat16
 
 
-def padded_2(value, sides, width):
-    for axis, dim in sides:
-        size, length = (lax.axis_size(axis), value.shape[dim])
-        up = [(i, (i + 1) % size) for i in range(size - 1)]
-        down = [(j, i) for i, j in up]
-        wide = width[dim]
-        last = lax.slice_in_dim(value, length - wide, length, axis=dim)
-        leading = lax.slice_in_dim(value, 0, wide, axis=dim)
-        before = lax.ppermute(last, axis, up)
-        after = lax.ppermute(leading, axis, down)
-        value = jnp.concatenate([before, value, after], axis=dim)
-    return value
+NEAR = ((-1, -1), (-1, 0), (-1, 1), (0, -1), (0, 1), (1, -1), (1, 0), (1, 1))
 
 
 SLOT = 24
@@ -31,10 +20,11 @@
 
 
 def compute_kernel(
-    shards,
+    down_count,
+    across,
     starts_ref,
     dims_ref,
-    tok_ref,
+    own_tok_ref,
     lat_ref,
     feat_ref,
     in_w_ref,
@@ -46,6 +36,14 @@
     up_b_ref,
     out_ref,
     weights,
+    tok_pack,
+    tok_all,
+    lat_rows,
+    lat_sides,
+    feat_rows,
+    feat_sides,
+    feat_corners,
+    row_pack,
     toks,
     rows_s,
     lat_s,
@@ -61,9 +59,29 @@
     upacc,
     out_s,
     sems,
+    tok_send,
+    tok_recv,
+    feat_send,
+    feat_recv,
+    lat_send,
+    lat_recv,
 ):
-    channels = in_b_ref.shape[1]
+    channels = in_b_ref.shape[0]
     lanes = 3 * channels
+    shards = down_count * across
+    ty = lax.axis_index("ty")
+    tx = lax.axis_index("tx")
+    myself = ty * across + tx
+    mesh_ids = pl.DeviceIdType.MESH
+
+    def peer(step):
+        other = lax.rem(myself + step, shards)
+        return {"ty": other // across, "tx": lax.rem(other, across)}
+
+    barrier = pltpu.get_barrier_semaphore()
+    for step in range(1, shards):
+        pl.semaphore_signal(barrier, inc=1, device_id=peer(step), device_id_type=mesh_ids)
+
     copies = []
     for f in range(3):
         for a in range(3):
@@ -74,8 +92,100 @@
             )
             copy.start()
             copies.append(copy)
-    row0 = lax.axis_index("ty") * 16
-    col0 = lax.axis_index("tx") * 32
+
+    token_rows = own_tok_ref.shape[1] // 128
+    tok_pack[...] = jnp.zeros_like(tok_pack)
+    for k in range(token_rows):
+        tok_pack[k : k + 1, :] = own_tok_ref[:, k * 128 : (k + 1) * 128].astype(F32)
+    tok_all[myself] = tok_pack[...].astype(BF16)
+
+    quarter = feat_ref.shape[2] // 4
+    pack_row = lax.broadcasted_iota(jnp.int32, (16, quarter), 0) // 2
+    for side in range(2):
+        packed = jnp.zeros((16, quarter), F32)
+        for k in range(4):
+            for f in range(2):
+                piece = feat_ref[f, :, k * quarter : (k + 1) * quarter].astype(F32)
+                turn = (4 * k + 2 * f - 14 * side) % 16
+                if turn:
+                    piece = pltpu.roll(piece, turn, axis=0)
+                packed = jnp.where(pack_row == 2 * k + f, piece, packed)
+        row_pack[side] = packed.astype(BF16)
+
+    pl.semaphore_wait(barrier, shards - 1)
+
+    def token_copy(step):
+        return pltpu.make_async_remote_copy(
+            src_ref=tok_all.at[myself],
+            dst_ref=tok_all.at[myself],
+            send_sem=tok_send.at[step],
+            recv_sem=tok_recv.at[step],
+            device_id=peer(step),
+            device_id_type=mesh_ids,
+        )
+
+    def token_arrival(step):
+        source = lax.rem(myself + shards - step, shards)
+        return pltpu.make_async_remote_copy(
+            src_ref=tok_all.at[source],
+            dst_ref=tok_all.at[source],
+            send_sem=tok_send.at[step],
+            recv_sem=tok_recv.at[step],
+            device_id=peer(step),
+            device_id_type=mesh_ids,
+        )
+
+    def near_copies(at, land, target):
+        dy, dx = NEAR[at]
+        side = (dy + 1) // 2
+        edge = 2 * channels
+        lat_piece = lat_ref.at[:, :, pl.ds(0 if dx < 0 else lat_ref.shape[2] - 128, 128)]
+        if dy == 0:
+            first = 0 if dx < 0 else feat_ref.shape[2] - edge
+            feat_pair = (feat_ref.at[:, :, pl.ds(first, edge)], feat_sides.at[land - 3])
+        elif dx == 0:
+            feat_pair = (row_pack.at[side], feat_rows.at[0 if land == 1 else 1])
+        else:
+            first = 0 if dx < 0 else quarter - edge
+            feat_pair = (row_pack.at[side, :, pl.ds(first, edge)], feat_corners.at[land])
+        if dx == 0:
+            lat_pair = (lat_ref, lat_rows.at[0 if land == 1 else 1])
+        else:
+            lat_pair = (lat_piece, lat_sides.at[land])
+        made = []
+        for (src, dst), send, recv in (
+            (feat_pair, feat_send, feat_recv),
+            (lat_pair, lat_send, lat_recv),
+        ):
+            made.append(
+                pltpu.make_async_remote_copy(
+                    src_ref=src,
+                    dst_ref=dst,
+                    send_sem=send.at[at],
+                    recv_sem=recv.at[land],
+                    device_id={"ty": ty + NEAR[target][0], "tx": tx + NEAR[target][1]},
+                    device_id_type=mesh_ids,
+                )
+            )
+        return made
+
+    def if_near(at, act):
+        dy, dx = NEAR[at]
+        there = (ty + dy >= 0) & (ty + dy < down_count) & (tx + dx >= 0) & (tx + dx < across)
+        pl.when(there)(act)
+
+    for step in range(1, shards):
+        token_copy(step).start()
+    for at in range(8):
+
+        def send_near(at=at):
+            for copy in near_copies(at, 7 - at, at):
+                copy.start()
+
+        if_near(at, send_near)
+
+    row0 = ty * 16
+    col0 = tx * 32
     height = dims_ref[0, 0]
     breadth = dims_ref[0, 1]
 
@@ -88,29 +198,38 @@
             )
 
     halves = (((0,), (1, 2)), ((0, 1), (2,)))
-
-    def up_sum(pr, ar, pc, ac):
-        total = None
-        for a in halves[pr][ar]:
-            for b in halves[pc][ac]:
-                at = (a * 3 + b) * channels
-                part = up_w_ref[at : at + channels, :].astype(F32)
-                total = part if total is None else total + part
-        return total
-
+    out_width = up_w_ref.shape[0]
     for pr in range(2):
         for ar in range(2):
-            near = jnp.concatenate([up_sum(pr, ar, 0, 1), up_sum(pr, ar, 1, 0)], axis=1)
-            far = jnp.concatenate([up_sum(pr, ar, 0, 0), up_sum(pr, ar, 1, 1)], axis=1)
-            upw[pr, ar * channels : (ar + 1) * channels, 0:channels] = near.astype(BF16)
-            upw[pr, ar * channels : (ar + 1) * channels, channels : 2 * channels] = far.astype(
-                BF16
-            )
-
-    token_rows = tok_ref.shape[1]
+            for part, (pc, ac) in enumerate(((0, 1), (1, 0), (0, 0), (1, 1))):
+                total = None
+                for a in halves[pr][ar]:
+                    for b in halves[pc][ac]:
+                        at = (a * 3 + b) * channels
+                        tap = up_w_ref[:, at : at + channels].astype(F32)
+                        total = tap if total is None else total + tap
+                upw[
+                    pr,
+                    part * out_width : (part + 1) * out_width,
+                    ar * channels : (ar + 1) * channels,
+                ] = total.astype(BF16)
+
+    for step in range(1, shards):
+        token_copy(step).wait_send()
+        token_arrival(step).wait_recv()
+    for at in range(8):
+
+        def wait_near(at=at):
+            for copy in near_copies(at, 7 - at, at):
+                copy.wait_send()
+            for copy in near_copies(7 - at, at, at):
+                copy.wait_recv()
+
+        if_near(at, wait_near)
+
     for j in range(shards):
-        toks[j] = jnp.zeros_like(toks[j])
-        toks[j, 8 : 8 + token_rows, :] = tok_ref[j].astype(F32)
+        toks[j, 0:8, :] = jnp.zeros((8, 128), F32)
+        toks[j, 8 : 8 + tok_all.shape[1], :] = tok_all[j].astype(F32)
     lane = lax.broadcasted_iota(jnp.int32, (8, 128), 1)
     token = lax.broadcasted_iota(jnp.int32, (8, 128), 0) * 8 + lane // 16
     rows_s[...] = jnp.zeros_like(rows_s)
@@ -141,7 +260,18 @@
     lat_row = lax.broadcasted_iota(jnp.int32, (HIGH, 640), 0) + (row0 - 8)
     lat_keep = (lat_row >= 0) & (lat_row < height) & (lat_col >= 0) & (lat_col < breadth)
     for f in range(2):
-        lat_s[f] = jnp.where(lat_keep, lat_ref[f].astype(F32), 0.0)
+        blocks = []
+        for west, centre, east in (
+            (lat_sides[0, f], lat_rows[0, f], lat_sides[2, f]),
+            (lat_sides[3, f], lat_ref[f], lat_sides[4, f]),
+            (lat_sides[5, f], lat_rows[1, f], lat_sides[7, f]),
+        ):
+            wide = jnp.concatenate(
+                [west.astype(F32), centre.astype(F32), east.astype(F32)], axis=1
+            )
+            blocks.append(pltpu.roll(wide, 768 - 80, axis=1)[:, :640])
+        tall = jnp.concatenate([blocks[0][8:16], blocks[1], blocks[2][0:8]], axis=0)
+        lat_s[f] = jnp.where(lat_keep, tall, 0.0)
     for g in range(5):
         lat_s[2, :, g * 128 : (g + 1) * 128] = rows_s[pl.ds(g, HIGH, stride=8), :]
 
@@ -176,18 +306,42 @@
         col = col0 - 2 + c
         return (col >= 0) & (col < breadth)
 
+    def packed_rows(rows_at, corner_at, f, c, land):
+        if c < 2:
+            col, lane0, held = 30 + c, c, feat_corners.at[corner_at]
+        elif c < 34:
+            col, lane0, held = c - 2, (c - 2) % 8, feat_rows.at[rows_at]
+        else:
+            col, lane0, held = c - 34, c - 34, feat_corners.at[corner_at + 2]
+        piece = held[:, lane0 * channels : (lane0 + 1) * channels].astype(F32)
+        turn = (land - (col // 8) * 4 - f * 2) % 16
+        if turn:
+            piece = pltpu.roll(piece, turn, axis=0)
+        return piece[0:8]
+
+    def feature_slab(f, c):
+        if c < 2:
+            middle = feat_sides[0, f, :, c * channels : (c + 1) * channels]
+        elif c < 34:
+            middle = feat_ref[f, :, (c - 2) * channels : (c - 1) * channels]
+        else:
+            middle = feat_sides[1, f, :, (c - 34) * channels : (c - 33) * channels]
+        above = packed_rows(0, 0, f, c, 6)
+        below = packed_rows(1, 5, f, c, 0)
+        return jnp.concatenate([above, middle.astype(F32), below], axis=0)
+
     tail = jnp.zeros((8, channels), F32)
     stage[36 * SLOT + 8 :, :] = jnp.zeros((stage.shape[0] - 36 * SLOT - 8, channels), F32)
     for f in range(2):
         before = tail
         for c in range(36):
-            slab = feat_ref[f, :, c * channels : (c + 1) * channels].astype(F32)
+            slab = feature_slab(f, c)
             slab = jnp.where(row_ok_near & col_ok(c), slab, 0.0)
             before = put_slab(stage, c, slab, before)
         stage[36 * SLOT : 36 * SLOT + 8, :] = before
         finish_lhs(f)
-    in_b = in_b_ref[...]
-    gain = gain_ref[...]
+    in_b = in_b_ref[...].reshape(1, channels)
+    gain = gain_ref[...].reshape(1, channels)
     before = tail
     before_values = tail
     for c in range(36):
@@ -222,7 +376,7 @@
 
     lax.fori_loop(0, 3, frame_dot, 0)
 
-    res_b = res_b_ref[...]
+    res_b = res_b_ref[...].reshape(1, channels)
     for c in range(34):
         rows = pl.ds(c * SLOT, HIGH)
         slab = acc[rows, channels : 2 * channels]
@@ -235,12 +389,15 @@
         grown[at : at + 16, channels : 2 * channels] = slab[8:24].astype(BF16)
         grown[at : at + 16, 2 * channels :] = pltpu.roll(slab, HIGH - 1, axis=0)[8:24].astype(BF16)
 
-    up_b = jnp.concatenate([up_b_ref[...], up_b_ref[...]], axis=1)
+    up_b = jnp.concatenate([up_b_ref[...].reshape(1, out_width)] * 2, axis=1)
     left = lax.broadcasted_iota(jnp.int32, (16, channels), 1) < channels // 2
     own_row = row_ok[8:24]
     for pr in range(2):
-        upacc[...] = jnp.dot(
-            grown[:, pr * channels : (pr + 2) * channels], upw[pr], preferred_element_type=F32
+        upacc[...] = lax.dot_general(
+            grown[:, pr * channels : (pr + 2) * channels],
+            upw[pr],
+            (((1,), (1,)), ((), ())),
+            preferred_element_type=F32,
         )
         for j in range(32):
             centre = upacc[(j + 1) * 16 : (j + 2) * 16, 0:channels]
@@ -251,30 +408,54 @@
             for k in range(channels // 128):
                 out_s[j * 3 + k, pl.ds(pr, 16, stride=2), :] = slab[:, k * 128 : (k + 1) * 128]
     for j in range(32 * 3):
-        out_ref[:, j * 128 : (j + 1) * 128] = out_s[j].astype(BF16)
-
-
-def compute(shards, starts, dims, tok, lat, feat, weights):
-    in_w, in_b, gain, res_w, res_b, up_w, up_b = weights
-    channels = in_b.shape[0]
-    out_width = up_b.shape[0]
+        out_ref[0, :, j * 128 : (j + 1) * 128] = out_s[j].astype(BF16)
+
+
+def per_device(
+    latent_shards,
+    shard_starts,
+    frame_dims,
+    latent_cache,
+    feature_cache,
+    in_weight,
+    in_bias,
+    norm_gain,
+    res_weight,
+    res_bias,
+    up_weight,
+    up_bias,
+):
+    channels = in_bias.shape[0]
+    out_width = up_bias.shape[0]
+    down_count = lax.axis_size("ty")
+    across = lax.axis_size("tx")
+    shards = down_count * across
+    token_rows = (latent_shards.shape[1] // 128 + 15) // 16 * 16
     cells = 34 * SLOT + 16
     vmem = pl.BlockSpec(memory_space=pltpu.VMEM)
     smem = pl.BlockSpec(memory_space=pltpu.SMEM)
     return pl.pallas_call(
-        functools.partial(compute_kernel, shards),
-        out_shape=jax.ShapeDtypeStruct((32, 64 * out_width), BF16),
+        functools.partial(compute_kernel, down_count, across),
+        out_shape=jax.ShapeDtypeStruct((1, 32, 64 * out_width), BF16),
         in_specs=[smem, smem, vmem, vmem, vmem, vmem, vmem, vmem]
         + [pl.BlockSpec(memory_space=pl.ANY), vmem, vmem, vmem],
         out_specs=vmem,
         scratch_shapes=[
             pltpu.VMEM((3, 3 * channels, 3 * channels), BF16),
-            pltpu.VMEM((shards, (tok.shape[1] + 16 + 15) // 8 * 8, 128), F32),
+            pltpu.VMEM((token_rows, 128), F32),
+            pltpu.VMEM((shards, token_rows, 128), BF16),
+            pltpu.VMEM((2, 2, 16, 512), BF16),
+            pltpu.VMEM((8, 2, 16, 128), BF16),
+            pltpu.VMEM((2, 16, 8 * channels), BF16),
+            pltpu.VMEM((2, 2, 16, 2 * channels), BF16),
+            pltpu.VMEM((8, 16, 2 * channels), BF16),
+            pltpu.VMEM((2, 16, 8 * channels), BF16),
+            pltpu.VMEM((shards, token_rows + 16, 128), F32),
             pltpu.VMEM((HIGH * 8, 128), F32),
             pltpu.VMEM((3, HIGH, 640), F32),
             pltpu.VMEM((9 * 128, 6 * channels), BF16),
             pltpu.VMEM((6 * HIGH, 9 * 128), BF16),
-            pltpu.VMEM((2, 2 * channels, 2 * channels), BF16),
+            pltpu.VMEM((2, 4 * out_width, 2 * channels), BF16),
             pltpu.VMEM((6 * HIGH, 6 * channels), F32),
             pltpu.VMEM((cells + 2 * SLOT, channels), F32),
             pltpu.VMEM((cells + 2 * SLOT, channels), F32),
@@ -284,47 +465,33 @@
             pltpu.VMEM((34 * 16, 2 * channels), F32),
             pltpu.VMEM((32 * 3, 32, 128), F32),
             pltpu.SemaphoreType.DMA((9,)),
+            pltpu.SemaphoreType.DMA((shards,)),
+            pltpu.SemaphoreType.DMA((shards,)),
+            pltpu.SemaphoreType.DMA((8,)),
+            pltpu.SemaphoreType.DMA((8,)),
+            pltpu.SemaphoreType.DMA((8,)),
+            pltpu.SemaphoreType.DMA((8,)),
         ],
-        compiler_params=pltpu.CompilerParams(vmem_limit_bytes=56 * 1024 * 1024),
+        compiler_params=pltpu.CompilerParams(
+            vmem_limit_bytes=56 * 1024 * 1024, collective_id=0, has_side_effects=True
+        ),
         cost_estimate=pl.CostEstimate(
             flops=9_000_000_000, bytes_accessed=13_000_000, transcendentals=400_000
         ),
     )(
-        starts,
-        dims,
-        tok,
-        lat,
-        feat,
-        in_w,
-        in_b.reshape(1, -1),
-        gain.reshape(1, -1),
-        res_w,
-        res_b.reshape(1, -1),
-        up_w,
-        up_b.reshape(1, -1),
+        shard_starts,
+        frame_dims,
+        latent_shards,
+        latent_cache[0],
+        feature_cache[0],
+        in_weight,
+        in_bias,
+        norm_gain,
+        res_weight,
+        res_bias,
+        up_weight.T,
+        up_bias,
     )
-
-
-def per_device(
-    latent_shards,
-    shard_starts,
-    frame_dims,
-    latent_cache,
-    feature_cache,
-    *weights,
-):
-    channels = weights[1].shape[0]
-    latent_width = weights[0].shape[0] // 27
-    shard_count = lax.axis_size("ty") * lax.axis_size("tx")
-    tok = lax.all_gather(latent_shards, ("ty", "tx"), axis=1, tiled=True)
-    tok = tok.reshape(shard_count, -1, 128)
-    sides = (("ty", 1), ("tx", 2))
-    lat = padded_2(latent_cache[0], sides, {1: 3, 2: 3 * latent_width})
-    lat = jnp.pad(lat, ((0, 0), (5, 5), (0, 32)))
-    feat = padded_2(feature_cache[0], sides, {1: 2, 2: 2 * channels})
-    feat = jnp.pad(feat, ((0, 0), (6, 6), (0, 0)))
-    out = compute(shard_count, shard_starts, frame_dims, tok, lat, feat, weights)
-    return out[None]
 
 
 def solution(mesh):

time: 70.1 us -> 32.7 us (0.47)
  starting transfers between devices: 20.9 us -> 0 us
  blocking collectives: 12.3 us -> 0 us
  Pallas kernels: 20.6 us -> 30.4 us
  local copies, waits for them, and re-layouts: 8.84 us -> 2.06 us
  other arithmetic: 3.74 us -> 0 us
  waiting for transfers between devices: 3 us -> 0 us
    ppermute x8 -> x0, starting transfers between devices: 20.9 us -> none  [the longest x4 14.5 us: padded_2(): before = lax.ppermute(last, axis, up)]
    all_gather x1 -> x0, blocking collectives: 12.3 us -> none  [per_device(): tok = lax.all_gather(latent_shards, ('ty', 'tx'), axis=1, tiled=True)]
    pallas_call x1, Pallas kernels: 20.6 us -> 30.4 us  [per_device(): pl.pallas_call(functools.partial(compute_kernel, down_count, across), out...]
    reshape x4 -> x0, local copies, waits for them, and re-layouts: 4.53 us -> none  [the longest x1 1.26 us: compute(): in_b.reshape(1, -1)]
    ppermute x8 -> x0, waiting for transfers between devices: 3 us -> none  [the longest x4 2.99 us: padded_2(): after = lax.ppermute(leading, axis, down)]
    concatenate x2 -> x0, other arithmetic: 2.41 us -> none  [padded_2(): value = jnp.concatenate([before, value, after], axis=dim)]
    slice x2 -> x0, local copies, waits for them, and re-layouts: 2.12 us -> none  [padded_2(): last = lax.slice_in_dim(value, length - wide, length, axis=dim)]
    all_gather x1 -> x0, other arithmetic: 1.18 us -> none  [per_device(): tok = lax.all_gather(latent_shards, ('ty', 'tx'), axis=1, tiled=True)]
  transfers between devices with their start and end apart: 8 -> 0, of which waited for: 1 -> 0; matrix products, arithmetic and copies ran while one was open for 14% -> 0% of each run, Pallas kernels for 0% -> 0%
where the time goes in v2:
time: 32.7 us; the launch traced here: 32.5 us
  Pallas kernels  30.4 us (93%)
  local copies, waits for them, and re-layouts  2.06 us (6%)
    pallas_call x1, Pallas kernels, per_device(): pl.pallas_call(functools.partial(compute_kernel, down_count, across), out...  30.4 us
    unnamed x1, local copies, waits for them, and re-layouts  2.06 us

profile of v2, /device:TPU:1, one launch (start us, length us, event | category | flops | bytes accessed | tf_op | source)
XLA Modules:
  0.0 32.5 jit_solution(1547044025937785429)
XLA Ops:
  0.0 30.4 %shard_map.118 = bf16[1,32,12288]{2,1,0:T(8,128)(2,1)} custom-call(s32[1,9]{1,0:T(1,128)} %starts_ref.1, s32[1,2]{1,0:T(1,128)} %dims_ref.1, bf16[1,12416]{1,0:T(2,128)(2,1)} %own_tok_ref.1, bf16[2,16,512]{2,1,0:T(8,128)(2,1)} %bitcast.5, bf16[2,16,12288]{2,1,0:T(8,128)(2,1)} %bitcast.4, bf16[432,384]{1,0:T(8,128)(2,1)} %in_w_ref.1, f32[384]{0:T(512)} %in_b_ref.1, ...), custom_call_target="tpu_custom_call" | custom-call | flops 8999999488 | bytes 13000000 | tf_op jit(solution)/shard_map/pallas_call | solution.py:437
  30.4 2.1 %copy.14 = bf16[1,32,12288]{2,1,0:T(8,128)(2,1)} copy(bf16[1,32,12288]{2,1,0:T(8,128)(2,1)} %shard_map.118) | data formatting | bytes 1572864

commit v3 on v2

--- a/solution.py
+++ b/solution.py
@@ -100,18 +100,6 @@
     tok_all[myself] = tok_pack[...].astype(BF16)
 
     quarter = feat_ref.shape[2] // 4
-    pack_row = lax.broadcasted_iota(jnp.int32, (16, quarter), 0) // 2
-    for side in range(2):
-        packed = jnp.zeros((16, quarter), F32)
-        for k in range(4):
-            for f in range(2):
-                piece = feat_ref[f, :, k * quarter : (k + 1) * quarter].astype(F32)
-                turn = (4 * k + 2 * f - 14 * side) % 16
-                if turn:
-                    piece = pltpu.roll(piece, turn, axis=0)
-                packed = jnp.where(pack_row == 2 * k + f, piece, packed)
-        row_pack[side] = packed.astype(BF16)
-
     pl.semaphore_wait(barrier, shards - 1)
 
     def token_copy(step):
@@ -176,13 +164,27 @@
 
     for step in range(1, shards):
         token_copy(step).start()
-    for at in range(8):
-
-        def send_near(at=at):
-            for copy in near_copies(at, 7 - at, at):
-                copy.start()
-
-        if_near(at, send_near)
+    def send_near(kind):
+        for at in range(8):
+
+            def send_one(at=at):
+                near_copies(at, 7 - at, at)[kind].start()
+
+            if_near(at, send_one)
+
+    send_near(1)
+    pack_row = lax.broadcasted_iota(jnp.int32, (16, quarter), 0) // 2
+    for side in range(2):
+        packed = jnp.zeros((16, quarter), F32)
+        for k in range(4):
+            for f in range(2):
+                piece = feat_ref[f, :, k * quarter : (k + 1) * quarter].astype(F32)
+                turn = (4 * k + 2 * f - 14 * side) % 16
+                if turn:
+                    piece = pltpu.roll(piece, turn, axis=0)
+                packed = jnp.where(pack_row == 2 * k + f, piece, packed)
+        row_pack[side] = packed.astype(BF16)
+    send_near(0)
 
     row0 = ty * 16
     col0 = tx * 32
@@ -217,15 +219,15 @@
     for step in range(1, shards):
         token_copy(step).wait_send()
         token_arrival(step).wait_recv()
-    for at in range(8):
-
-        def wait_near(at=at):
-            for copy in near_copies(at, 7 - at, at):
-                copy.wait_send()
-            for copy in near_copies(7 - at, at, at):
-                copy.wait_recv()
-
-        if_near(at, wait_near)
+    def wait_near(kind):
+        for at in range(8):
+
+            def wait_one(at=at):
+                near_copies(at, 7 - at, at)[kind].wait_send()
+                near_copies(7 - at, at, at)[kind].wait_recv()
+
+            if_near(at, wait_one)
+
 
     for j in range(shards):
         toks[j, 0:8, :] = jnp.zeros((8, 128), F32)
@@ -255,6 +257,7 @@
         return carry
 
     lax.fori_loop(5, 27, one_row, 0)
+    wait_near(1)
     lat_lane = lax.broadcasted_iota(jnp.int32, (HIGH, 640), 1)
     lat_col = lat_lane // 16 + (col0 - 3)
     lat_row = lax.broadcasted_iota(jnp.int32, (HIGH, 640), 0) + (row0 - 8)
@@ -332,14 +335,6 @@
 
     tail = jnp.zeros((8, channels), F32)
     stage[36 * SLOT + 8 :, :] = jnp.zeros((stage.shape[0] - 36 * SLOT - 8, channels), F32)
-    for f in range(2):
-        before = tail
-        for c in range(36):
-            slab = feature_slab(f, c)
-            slab = jnp.where(row_ok_near & col_ok(c), slab, 0.0)
-            before = put_slab(stage, c, slab, before)
-        stage[36 * SLOT : 36 * SLOT + 8, :] = before
-        finish_lhs(f)
     in_b = in_b_ref[...].reshape(1, channels)
     gain = gain_ref[...].reshape(1, channels)
     before = tail
@@ -360,21 +355,22 @@
 
     for copy in copies:
         copy.wait()
+    acc[...] = jnp.dot(lhs[2], weights[2], preferred_element_type=F32)
+    wait_near(0)
+    for f in range(2):
+        before = tail
+        for c in range(36):
+            slab = feature_slab(f, c)
+            slab = jnp.where(row_ok_near & col_ok(c), slab, 0.0)
+            before = put_slab(stage, c, slab, before)
+        stage[36 * SLOT : 36 * SLOT + 8, :] = before
+        finish_lhs(f)
 
     def frame_dot(f, carry):
-        part = jnp.dot(lhs[f], weights[f], preferred_element_type=F32)
-
-        @pl.when(f == 0)
-        def _():
-            acc[...] = part
-
-        @pl.when(f > 0)
-        def _():
-            acc[...] += part
-
+        acc[...] += jnp.dot(lhs[f], weights[f], preferred_element_type=F32)
         return carry
 
-    lax.fori_loop(0, 3, frame_dot, 0)
+    lax.fori_loop(0, 2, frame_dot, 0)
 
     res_b = res_b_ref[...].reshape(1, channels)
     for c in range(34):

time: 32.7 us -> 29.1 us (0.89)
  Pallas kernels: 30.4 us -> 26.8 us
    pallas_call x1, Pallas kernels: 30.4 us -> 26.8 us  [per_device(): pl.pallas_call(functools.partial(compute_kernel, down_count, across), out...]
where the time goes in v3:
time: 29.1 us; the launch traced here: 28.9 us
  Pallas kernels  26.8 us (92%)
  local copies, waits for them, and re-layouts  2.06 us (7%)
    pallas_call x1, Pallas kernels, per_device(): pl.pallas_call(functools.partial(compute_kernel, down_count, across), out...  26.8 us
    unnamed x1, local copies, waits for them, and re-layouts  2.06 us

profile of v3, /device:TPU:1, one launch (start us, length us, event | category | flops | bytes accessed | tf_op | source)
XLA Modules:
  0.0 28.9 jit_solution(3655584441081353012)
XLA Ops:
  0.0 26.8 %shard_map.118 = bf16[1,32,12288]{2,1,0:T(8,128)(2,1)} custom-call(s32[1,9]{1,0:T(1,128)} %starts_ref.1, s32[1,2]{1,0:T(1,128)} %dims_ref.1, bf16[1,12416]{1,0:T(2,128)(2,1)} %own_tok_ref.1, bf16[2,16,512]{2,1,0:T(8,128)(2,1)} %bitcast.5, bf16[2,16,12288]{2,1,0:T(8,128)(2,1)} %bitcast.4, bf16[432,384]{1,0:T(8,128)(2,1)} %in_w_ref.1, f32[384]{0:T(512)} %in_b_ref.1, ...), custom_call_target="tpu_custom_call" | custom-call | flops 8999999488 | bytes 13000000 | tf_op jit(solution)/shard_map/pallas_call | solution.py:433
  26.8 2.1 %copy.14 = bf16[1,32,12288]{2,1,0:T(8,128)(2,1)} copy(bf16[1,32,12288]{2,1,0:T(8,128)(2,1)} %shard_map.118) | data formatting | bytes 1572864
